TPU v7x, 256 devices: a whole 4x4x8 slice. The times are simulated.
256 devices in a mesh: ctx: 64 (over y, z, core), head: 4 (over x).
Axes of the slice: x: 4, y: 4, z: 8, core: 2. Of those that a mesh axis runs over, the one named last changes fastest.
Arguments:
- queries: bfloat16 [16384, 64, 128], P('ctx', 'head'), may hold values from -120 to 120
- keys: bfloat16 [16384, 8, 128], P('ctx', 'head'), may hold values from -7 to 7
- values: bfloat16 [16384, 8, 128], P('ctx', 'head'), may hold values from -6 to 6
- doc_lengths: int32 [32], replicated, may hold values from 1 to 1280, 16384 in all
Outputs:
- attended: bfloat16 [16384, 64, 128], P(('ctx', 'head'))
Inputs may be any that keep to these rules, and one draw needn't show every extreme that they name: `doc_lengths`: the lengths sum to 16384; the longest is exactly 1280.
All inputs are finite; a program needn't handle non-finite values.
Results may differ from a plain program's by a relative error of at most 0.005.
Values may be sent and summed in bfloat16 or wider, within the bound.
A program may use at most 64 MiB of HBM per device.

v0:
```python
from functools import partial
import math

import jax
import jax.numpy as jnp
from jax import lax
from jax.sharding import PartitionSpec as P

REACH = 5


def shifted(shard, axis, by):
    size = lax.axis_size(axis)
    pairs = [(i, i + by) for i in range(size) if 0 <= i + by < size]
    return lax.ppermute(shard, axis, pairs)


def absorb(query_group, key_block, value_block, allowed, score_scale, carried):
    maximum, denom_sum, weighted = carried
    scores = (
        jnp.einsum("qjd,kd->jqk", query_group, key_block, preferred_element_type=jnp.float32)
        * score_scale
    )
    scores = jnp.where(allowed[None], scores, -jnp.inf)
    new_max = jnp.maximum(maximum, jnp.max(scores, axis=-1))
    factor = jnp.exp(maximum - new_max)
    weights = jnp.exp(scores - new_max[..., None])
    denom_sum = denom_sum * factor + jnp.sum(weights, axis=-1)
    weighted = weighted * factor[..., None] + jnp.einsum(
        "jqk,kd->jqd", weights.astype(jnp.bfloat16), value_block, preferred_element_type=jnp.float32
    )
    return (new_max, denom_sum, weighted)


def local(queries, keys, values, doc_lengths):
    row_count = queries.shape[0]
    group_count = keys.shape[1]
    per_group = queries.shape[1] // group_count
    head_size = queries.shape[2]
    score_scale = 1.0 / math.sqrt(head_size)
    shard_index = lax.axis_index("ctx")
    offsets = jnp.cumsum(doc_lengths) - doc_lengths
    positions = jnp.arange(row_count, dtype=jnp.int32)
    query_pos = shard_index * row_count + positions
    doc_start = jnp.max(
        jnp.where(offsets[None, :] <= query_pos[:, None], offsets[None, :], 0), axis=1
    )
    paired = jnp.stack((keys, values))
    blocks_held = [paired]
    current = paired
    for step_index in range(REACH):
        current = shifted(current, "ctx", 1)
        blocks_held.append(current)
    results = []
    for group_index in range(group_count):
        query_group = queries[:, group_index * per_group : (group_index + 1) * per_group, :]
        carried = (
            jnp.full((per_group, row_count), -jnp.inf, jnp.float32),
            jnp.zeros((per_group, row_count), jnp.float32),
            jnp.zeros((per_group, row_count, head_size), jnp.float32),
        )
        for lag_index in range(REACH + 1):
            key_pos = (shard_index - lag_index) * row_count + positions
            allowed = (key_pos[None, :] <= query_pos[:, None]) & (
                key_pos[None, :] >= doc_start[:, None]
            )
            key_block = blocks_held[lag_index][0, :, group_index, :]
            value_block = blocks_held[lag_index][1, :, group_index, :]
            absorb_block = partial(
                absorb, query_group, key_block, value_block, allowed, score_scale
            )
            carried = absorb_block(carried)
        maximum, denom_sum, weighted = carried
        finished = weighted / denom_sum[:, :, None]
        results.append(jnp.transpose(finished, (1, 0, 2)))
    attended = jnp.concatenate(results, axis=1).astype(jnp.bfloat16)
    return lax.all_to_all(attended, "head", split_axis=0, concat_axis=1, tiled=True)


def solution(mesh):
    in_specs = (P("ctx", "head", None), P("ctx", "head", None), P("ctx", "head", None), P())
    out_specs = P(("ctx", "head"), None, None)
    return jax.shard_map(local, mesh=mesh, in_specs=in_specs, out_specs=out_specs, check_vma=False)
```

profile of v0, /device:TPU:24, one launch (start us, length us, event | category | flops | bytes accessed | tf_op | source)
XLA Modules:
  0.0 81.6 jit_solution(4406059094715977743)
XLA Ops:
  0.0 1.0 %copy_bitcast_fusion = (bf16[1,256,2,128]{3,1,2,0:T(8,128)(2,1)S(1)}, bf16[1,256,2,128]{3,1,2,0:T(8,128)(2,1)S(1)}) fusion(bf16[256,2,128]{2,1,0:T(2,128)(2,1)} %param.6, bf16[256,2,128]{2,1,0:T(2,128)(2,1)} %param.5), kind=kLoop, calls=%fused_computation.118 | loop fusion | bytes 524288 | tf_op jit(solution)/shard_map/stack | solution.py:48
  1.0 1.9 %collective-permute-start = (bf16[2,256,2,128]{3,1,2,0:T(8,128)(2,1)S(1)}, bf16[2,256,2,128]{3,1,2,0:T(8,128)(2,1)S(1)}, u32[]{:S(2)}, u32[]{:S(2)}) collective-permute-start(bf16[2,256,2,128]{3,1,2,0:T(8,128)(2,1)S(1)} %pad_maximum_fusion.1), channel_id=1, source_target_pairs={{0,4},{4,8},{8,12},{12,16},{16,20},{20,24},{24,28},{28,32},{32,36}... | collective-permute-start | bytes 786440 | tf_op jit(solution)/shard_map/ppermute | solution.py:15
  3.0 0.7 copy.60
  3.9 0.7 sub.263
  4.5 1.3 %fusion.110 = (bf16[256,8,128]{2,1,0:T(8,128)(2,1)S(1)}, bf16[256,8,128]{2,1,0:T(8,128)(2,1)S(1)}) fusion(bf16[256,16,128]{2,1,0:T(8,128)(2,1)} %param.4), kind=kLoop, calls=%fused_computation.203 | loop fusion | bytes 2097152 | tf_op jit(solution)/shard_map/slice | solution.py:56
  5.9 0.4 compare_and_fusion.4
  6.3 0.5 fusion.117
  6.8 0.5 fusion.111
  7.3 0.3 fusion
  7.9 4.6 %collective-permute-done = bf16[2,256,2,128]{3,1,2,0:T(8,128)(2,1)S(1)} collective-permute-done((bf16[2,256,2,128]{3,1,2,0:T(8,128)(2,1)S(1)}, bf16[2,256,2,128]{3,1,2,0:T(8,128)(2,1)S(1)}, u32[]{:S(2)}, u32[]{:S(2)}) %collective-permute-start) | collective-permute-done | bytes 262176 | tf_op jit(solution)/shard_map/ppermute | solution.py:15
  12.5 1.9 %collective-permute-start.1 = (bf16[2,256,2,128]{3,1,2,0:T(8,128)(2,1)S(1)}, bf16[2,256,2,128]{3,1,2,0:T(8,128)(2,1)S(1)}, u32[]{:S(2)}, u32[]{:S(2)}) collective-permute-start(bf16[2,256,2,128]{3,1,2,0:T(8,128)(2,1)S(1)} %collective-permute-done), channel_id=1, source_target_pairs={{0,4},{4,8},{8,12},{12,16},{16,20},{20,24},{24,28},{28,32},{32,36}... | collective-permute-start | bytes 786440 | tf_op jit(solution)/shard_map/ppermute | solution.py:15
  14.4 0.5 fusion.122
  14.9 0.5 fusion.116
  15.3 6.9 %collective-permute-done.1 = bf16[2,256,2,128]{3,1,2,0:T(8,128)(2,1)S(1)} collective-permute-done((bf16[2,256,2,128]{3,1,2,0:T(8,128)(2,1)S(1)}, bf16[2,256,2,128]{3,1,2,0:T(8,128)(2,1)S(1)}, u32[]{:S(2)}, u32[]{:S(2)}) %collective-permute-start.1) | collective-permute-done | bytes 262176 | tf_op jit(solution)/shard_map/ppermute | solution.py:15
  22.3 1.9 %collective-permute-start.2 = (bf16[2,256,2,128]{3,1,2,0:T(8,128)(2,1)S(1)}, bf16[2,256,2,128]{3,1,2,0:T(8,128)(2,1)S(1)}, u32[]{:S(2)}, u32[]{:S(2)}) collective-permute-start(bf16[2,256,2,128]{3,1,2,0:T(8,128)(2,1)S(1)} %collective-permute-done.1), channel_id=1, source_target_pairs={{0,4},{4,8},{8,12},{12,16},{16,20},{20,24},{24,28},{28,32},{32,36}... | collective-permute-start | bytes 786440 | tf_op jit(solution)/shard_map/ppermute | solution.py:15
  24.2 0.5 fusion.121
  24.7 0.5 fusion.115
  25.2 6.9 %collective-permute-done.2 = bf16[2,256,2,128]{3,1,2,0:T(8,128)(2,1)S(1)} collective-permute-done((bf16[2,256,2,128]{3,1,2,0:T(8,128)(2,1)S(1)}, bf16[2,256,2,128]{3,1,2,0:T(8,128)(2,1)S(1)}, u32[]{:S(2)}, u32[]{:S(2)}) %collective-permute-start.2) | collective-permute-done | bytes 262176 | tf_op jit(solution)/shard_map/ppermute | solution.py:15
  32.1 1.9 %collective-permute-start.3 = (bf16[2,256,2,128]{3,1,2,0:T(8,128)(2,1)S(1)}, bf16[2,256,2,128]{3,1,2,0:T(8,128)(2,1)S(1)}, u32[]{:S(2)}, u32[]{:S(2)}) collective-permute-start(bf16[2,256,2,128]{3,1,2,0:T(8,128)(2,1)S(1)} %collective-permute-done.2), channel_id=1, source_target_pairs={{0,4},{4,8},{8,12},{12,16},{16,20},{20,24},{24,28},{28,32},{32,36}... | collective-permute-start | bytes 786440 | tf_op jit(solution)/shard_map/ppermute | solution.py:15
  34.0 0.5 fusion.120
  34.4 0.5 fusion.114
  34.9 6.9 %collective-permute-done.3 = bf16[2,256,2,128]{3,1,2,0:T(8,128)(2,1)S(1)} collective-permute-done((bf16[2,256,2,128]{3,1,2,0:T(8,128)(2,1)S(1)}, bf16[2,256,2,128]{3,1,2,0:T(8,128)(2,1)S(1)}, u32[]{:S(2)}, u32[]{:S(2)}) %collective-permute-start.3) | collective-permute-done | bytes 262176 | tf_op jit(solution)/shard_map/ppermute | solution.py:15
  41.8 2.1 %collective-permute-start.4 = (bf16[2,256,2,128]{3,1,2,0:T(8,128)(2,1)S(1)}, bf16[2,256,2,128]{3,1,2,0:T(8,128)(2,1)S(1)}, u32[]{:S(2)}, u32[]{:S(2)}) collective-permute-start(bf16[2,256,2,128]{3,1,2,0:T(8,128)(2,1)S(1)} %collective-permute-done.3), channel_id=1, source_target_pairs={{0,4},{4,8},{8,12},{12,16},{16,20},{20,24},{24,28},{28,32},{32,36}... | collective-permute-start | bytes 786440 | tf_op jit(solution)/shard_map/ppermute | solution.py:15
  43.9 0.5 fusion.119
  44.4 0.5 fusion.113
  44.9 6.7 %collective-permute-done.4 = bf16[2,256,2,128]{3,1,2,0:T(8,128)(2,1)S(1)} collective-permute-done((bf16[2,256,2,128]{3,1,2,0:T(8,128)(2,1)S(1)}, bf16[2,256,2,128]{3,1,2,0:T(8,128)(2,1)S(1)}, u32[]{:S(2)}, u32[]{:S(2)}) %collective-permute-start.4) | collective-permute-done | bytes 262176 | tf_op jit(solution)/shard_map/ppermute | solution.py:15
  51.6 0.5 fusion.118
  52.4 0.3 fusion.4
  53.0 0.3 fusion.8
  53.7 0.9 %fusion.47 = f32[256,8,128]{2,0,1:T(8,128)S(1)} fusion(f32[8,256,256]{1,2,0:T(8,128)S(1)} %get-tuple-element.52, f32[8,256]{1,0:T(8,128)S(1)} %get-tuple-element.51, f32[256,8]{0,1:T(8,128)S(1)} %get-tuple-element.10, f32[256,8]{0,1:T(8,128)S(1)} %get-tuple-element.29, bf16[1,256,2,128]{3,1,2,0:T(8,128)(2,1)S(1)} %get-tuple-element.69), kind=kOutput, calls=%fused_computation.83 | convolution fusion | flops 135790592 | bytes 3235840 | tf_op jit(solution)/shard_map/jqk,kd->jqd/dot_general | solution.py:29
  54.6 0.5 fusion.112
  55.1 0.3 fusion.14
  56.0 0.3 fusion.20
  56.3 0.3 fusion.22
  56.6 0.9 %fusion.35 = f32[256,8,128]{2,0,1:T(8,128)S(1)} fusion(f32[8,256,256]{1,2,0:T(8,128)S(1)} %get-tuple-element.40, f32[8,256]{1,0:T(8,128)S(1)} %get-tuple-element.39, f32[256,8]{0,1:T(8,128)S(1)} %get-tuple-element.21, f32[256,8]{0,1:T(8,128)S(1)} %get-tuple-element.31, bf16[1,256,2,128]{3,1,2,0:T(8,128)(2,1)S(1)} %get-tuple-element.69), kind=kOutput, calls=%fused_computation.65 | convolution fusion | flops 135790592 | bytes 3235840 | tf_op jit(solution)/shard_map/jqk,kd->jqd/dot_general | solution.py:29
  57.5 0.7 fusion.45
  58.2 0.7 fusion.43
  58.9 0.7 fusion.41
  59.6 0.7 fusion.39
  60.2 0.7 fusion.48
  60.9 0.7 fusion.33
  61.6 0.7 fusion.31
  62.2 0.9 %fusion.29 = f32[256,8,128]{2,0,1:T(8,128)S(1)} fusion(f32[256,8,128]{2,0,1:T(8,128)S(1)} %fusion.31, f32[8,256,256]{1,2,0:T(8,128)S(1)} %get-tuple-element.46, f32[8,256]{1,0:T(8,128)S(1)} %get-tuple-element.24, f32[256,8]{0,1:T(8,128)S(1)} %get-tuple-element.18, bf16[2,256,2,128]{3,1,2,0:T(8,128)(2,1)S(1)} %collective-permute-done.2), kind=kOutput, calls=%fused_computation.56 | convolution fusion | flops 135790592 | bytes 4276224 | tf_op jit(solution)/shard_map/jqk,kd->jqd/dot_general | solution.py:29
  63.1 0.7 fusion.27
  63.8 0.7 fusion.49
  64.6 0.7 copy.77
  65.3 15.0 %all_to_all.18 = bf16[256,16,128]{2,1,0:T(8,128)(2,1)S(1)} all-to-all(bf16[256,16,128]{2,1,0:T(8,128)(2,1)S(1)} %copy.77), channel_id=1, replica_groups=mesh['ctx'=64,'head'=4] {'head'}, dimensions={0} | all-to-all | bytes 2097152 | tf_op jit(solution)/shard_map/all_to_all | solution.py:77
  80.3 1.3 %copy.78 = bf16[64,4,16,128]{3,2,1,0:T(8,128)(2,1)} copy(bf16[64,4,16,128]{3,2,0,1:T(8,128)(2,1)S(1)} %bitcast.425) | data formatting | bytes 2097152 | tf_op jit(solution)/shard_map/all_to_all | solution.py:77
  (20 shorter events, 2.3 us)
Async XLA Ops:
  1.0 11.4 %collective-permute-start = (bf16[2,256,2,128]{3,1,2,0:T(8,128)(2,1)S(1)}, bf16[2,256,2,128]{3,1,2,0:T(8,128)(2,1)S(1)}, u32[]{:S(2)}, u32[]{:S(2)}) collective-permute-start(bf16[2,256,2,128]{3,1,2,0:T(8,128)(2,1)S(1)} %pad_maximum_fusion.1), channel_id=1, source_target_pairs={{0,4},{4,8},{8,12},{12,16},{16,20},{20,24},{24,28},{28,32},{32,36}... | collective-permute-start | bytes 786440 | tf_op jit(solution)/shard_map/ppermute | solution.py:15
  12.5 9.8 %collective-permute-start.1 = (bf16[2,256,2,128]{3,1,2,0:T(8,128)(2,1)S(1)}, bf16[2,256,2,128]{3,1,2,0:T(8,128)(2,1)S(1)}, u32[]{:S(2)}, u32[]{:S(2)}) collective-permute-start(bf16[2,256,2,128]{3,1,2,0:T(8,128)(2,1)S(1)} %collective-permute-done), channel_id=1, source_target_pairs={{0,4},{4,8},{8,12},{12,16},{16,20},{20,24},{24,28},{28,32},{32,36}... | collective-permute-start | bytes 786440 | tf_op jit(solution)/shard_map/ppermute | solution.py:15
  22.3 9.8 %collective-permute-start.2 = (bf16[2,256,2,128]{3,1,2,0:T(8,128)(2,1)S(1)}, bf16[2,256,2,128]{3,1,2,0:T(8,128)(2,1)S(1)}, u32[]{:S(2)}, u32[]{:S(2)}) collective-permute-start(bf16[2,256,2,128]{3,1,2,0:T(8,128)(2,1)S(1)} %collective-permute-done.1), channel_id=1, source_target_pairs={{0,4},{4,8},{8,12},{12,16},{16,20},{20,24},{24,28},{28,32},{32,36}... | collective-permute-start | bytes 786440 | tf_op jit(solution)/shard_map/ppermute | solution.py:15
  32.1 9.8 %collective-permute-start.3 = (bf16[2,256,2,128]{3,1,2,0:T(8,128)(2,1)S(1)}, bf16[2,256,2,128]{3,1,2,0:T(8,128)(2,1)S(1)}, u32[]{:S(2)}, u32[]{:S(2)}) collective-permute-start(bf16[2,256,2,128]{3,1,2,0:T(8,128)(2,1)S(1)} %collective-permute-done.2), channel_id=1, source_target_pairs={{0,4},{4,8},{8,12},{12,16},{16,20},{20,24},{24,28},{28,32},{32,36}... | collective-permute-start | bytes 786440 | tf_op jit(solution)/shard_map/ppermute | solution.py:15
  41.8 9.8 %collective-permute-start.4 = (bf16[2,256,2,128]{3,1,2,0:T(8,128)(2,1)S(1)}, bf16[2,256,2,128]{3,1,2,0:T(8,128)(2,1)S(1)}, u32[]{:S(2)}, u32[]{:S(2)}) collective-permute-start(bf16[2,256,2,128]{3,1,2,0:T(8,128)(2,1)S(1)} %collective-permute-done.3), channel_id=1, source_target_pairs={{0,4},{4,8},{8,12},{12,16},{16,20},{20,24},{24,28},{28,32},{32,36}... | collective-permute-start | bytes 786440 | tf_op jit(solution)/shard_map/ppermute | solution.py:15
where the time goes:
time: 81.8 us; the launch traced here: 81.6 us
  waiting for transfers between devices  32 us (39%)
  blocking collectives  15 us (18%)
  matrix products  14.3 us (17%)
  starting transfers between devices  9.74 us (12%)
  other arithmetic  5.1 us (6%)
  local copies, waits for them, and re-layouts  4.98 us (6%)
    ppermute x5, waiting for transfers between devices, shifted(): return lax.ppermute(shard, axis, pairs)  32 us
    all_to_all x1, blocking collectives, local(): lax.all_to_all(attended, 'head', split_axis=0, concat_axis=1, tiled=True)  15 us
    ppermute x5, starting transfers between devices, shifted(): return lax.ppermute(shard, axis, pairs)  9.74 us
    dot_general x12, matrix products, absorb(): jnp.einsum('jqk,kd->jqd', weights.astype(jnp.bfloat16), value_block, pref...  8.68 us
    dot_general x12, matrix products, absorb(): jnp.einsum('qjd,kd->jqk', query_group, key_block, preferred_element_type=...  5.64 us
    reduce_sum x12, other arithmetic, absorb(): denom_sum = denom_sum * factor + jnp.sum(weights, axis=-1)  3.57 us
  transfers between devices with their start and end apart: 5, of which 5 were waited for; matrix products, arithmetic and copies ran while one was open for 11% of the time, Pallas kernels for 0%

commit v1 on v0

v1 whole, which is shorter than its diff:
```python
import functools
import math

import jax
import jax.numpy as jnp
from jax import lax
from jax.experimental import pallas as pl
from jax.experimental.pallas import tpu as pltpu
from jax.sharding import PartitionSpec as P

MESH = pl.DeviceIdType.MESH
LAGS = 6
LANES = 128
MASKED = -1e30
TILE = 256


def kernel(
    nc, nh, dl_ref, q_ref, kv_ref, out_ref,
    qe, msk, kvb, acc, mst, obuf, rbuf,
    zs_sem, ss_sem, kr_sem, as_sem, ar_sem,
):
    rows, heads, width = q_ref.shape
    groups = kv_ref.shape[0]
    per = heads // groups
    docs = dl_ref.shape[0]
    part = rows // nh
    tokens = TILE // per
    scale = math.log2(math.e) / math.sqrt(width)
    me = lax.axis_index("ctx")
    mh = lax.axis_index("head")
    core = lax.rem(me, 2)
    sib = me + 1 - 2 * core

    def at(by):
        return lax.rem(me + by + nc, nc)

    def head_at(by):
        return lax.rem(mh + by, nh)

    barrier = pltpu.get_barrier_semaphore()

    def greet(dev):
        pl.semaphore_signal(barrier, inc=1, device_id=dev, device_id_type=MESH)

    greet((at(-2), mh))
    greet((sib, mh))
    for by in range(1, nh):
        greet((me, head_at(by)))

    @pl.when(core == 0)
    def _():
        greet((at(-1), mh))

    pl.semaphore_wait(barrier, nh + 1 + core)

    def source(g, lag):
        return kv_ref.at[g] if lag == 0 else kvb.at[g, lag - 1]

    def along(g, lag):
        return pltpu.make_async_remote_copy(
            src_ref=source(g, lag), dst_ref=kvb.at[g, lag + 1],
            send_sem=zs_sem.at[g, lag // 2], recv_sem=kr_sem.at[g, lag + 1],
            device_id=(at(2), mh), device_id_type=MESH)

    def across(g):
        return pltpu.make_async_remote_copy(
            src_ref=source(g, 4), dst_ref=kvb.at[g, 4],
            send_sem=zs_sem.at[g, 2], recv_sem=kr_sem.at[g, 4],
            device_id=(at(1), mh), device_id_type=MESH)

    def beside(g, lag):
        there = lag - 2 * core
        return pltpu.make_async_remote_copy(
            src_ref=source(g, lag), dst_ref=kvb.at[g, there],
            send_sem=ss_sem.at[g, lag // 2], recv_sem=kr_sem.at[g, there],
            device_id=(sib, mh), device_id_type=MESH)

    def on_core(which, do):
        @pl.when(core == which)
        def _():
            do()

    def arrive(g, lag):
        slot = kvb.at[g, lag - 1]
        pltpu.make_async_remote_copy(
            src_ref=slot, dst_ref=slot, send_sem=zs_sem.at[g, 0], recv_sem=kr_sem.at[g, lag - 1],
            device_id=(sib, mh), device_id_type=MESH).wait_recv()

    for g in range(groups):
        along(g, 0).start()
        on_core(0, lambda g=g: beside(g, 0).start())

    lane = lax.broadcasted_iota(jnp.int32, (8, LANES), 1)
    starts = jnp.full((8, LANES), 1 << 30, jnp.int32)
    ends = jnp.zeros((8, LANES), jnp.int32)
    total = jnp.int32(0)
    for d in range(docs):
        upto = total + dl_ref[d]
        starts = jnp.where(lane == d, total, starts)
        ends = jnp.where(lane == d, upto, ends)
        total = upto
    starts, ends = starts[0:1], ends[0:1]

    for lag in range(LAGS):
        pos = (me - lag) * rows + lax.broadcasted_iota(jnp.int32, (rows, LANES), 0)
        inside = (pos >= starts) & (pos < ends)
        msk[lag] = jnp.where(inside, 0.0, MASKED).astype(jnp.bfloat16)

    def gather_queries(r, _):
        first = pl.multiple_of(r * tokens, tokens)
        at_row = pl.multiple_of(r * TILE, TILE)
        x = q_ref[pl.ds(first, tokens)].astype(jnp.float32)
        pos = me * rows + first + lax.broadcasted_iota(jnp.int32, (tokens, per, LANES), 0)
        inside = (pos >= starts[None]) & (pos < ends[None])
        hot = jnp.where(inside, 1.0, 0.0).reshape(TILE, LANES).astype(jnp.bfloat16)
        for g in range(groups):
            qg = x[:, g * per:(g + 1) * per, :].reshape(TILE, width).astype(jnp.bfloat16)
            qe[g, pl.ds(at_row, TILE), 0:width] = qg
            qe[g, pl.ds(at_row, TILE), width:2 * width] = hot
        return 0

    lax.fori_loop(0, rows // tokens, gather_queries, 0)

    ones = jnp.ones((rows, width), jnp.bfloat16)

    def attend(g, r, lags, first, last):
        at_row = pl.multiple_of(r * TILE, TILE)
        q = qe[g, pl.ds(at_row, TILE), :]
        scores = []
        for lag in lags:
            ref = source(g, lag)
            k = jnp.concatenate([ref[0], msk[lag]], axis=1)
            s = lax.dot_general(q, k, (((1,), (1,)), ((), ())), preferred_element_type=jnp.float32)
            if lag == 0:
                tok = r * tokens + lax.broadcasted_iota(jnp.int32, (tokens, per, rows), 0)
                key = lax.broadcasted_iota(jnp.int32, (tokens, per, rows), 2)
                s = jnp.where(key <= tok, s.reshape(tokens, per, rows), MASKED).reshape(TILE, rows)
            scores.append(s)
        top = functools.reduce(jnp.maximum, scores)
        top = jnp.max(top, axis=1, keepdims=True)
        if not first:
            before = mst[g, pl.ds(at_row, TILE), :]
            top = jnp.maximum(before, top)
        else:
            top = jnp.broadcast_to(top, (TILE, LANES))
        low = top * scale
        low2 = jnp.concatenate([low] * (rows // LANES), axis=1)
        mixed = None
        for lag, s in zip(lags, scores):
            w = jnp.exp2(s * scale - low2).astype(jnp.bfloat16)
            v = jnp.concatenate([source(g, lag)[1], ones], axis=1)
            out = jnp.dot(w, v, preferred_element_type=jnp.float32)
            mixed = out if mixed is None else mixed + out
        if not first:
            fade = jnp.exp2(before * scale - low)
            mixed = mixed + acc[g, pl.ds(at_row, TILE), :] * jnp.concatenate([fade, fade], axis=1)
        if not last:
            mst[g, pl.ds(at_row, TILE), :] = top
            acc[g, pl.ds(at_row, TILE), :] = mixed
            return None
        return (mixed[:, :width] / mixed[:, width:]).astype(jnp.bfloat16)

    def sweep(g, lags, first):
        def body(r, _):
            attend(g, r, lags, first, False)
            return 0
        lax.fori_loop(0, rows * per // TILE, body, 0)

    def give(g, to):
        return pltpu.make_async_remote_copy(
            src_ref=obuf.at[g, to], dst_ref=rbuf.at[g, mh],
            send_sem=as_sem.at[g, to], recv_sem=ar_sem.at[g, mh],
            device_id=(me, to), device_id_type=MESH)

    per_part = part * per // TILE

    def finish(g, lags):
        def chunk(k, _):
            to = head_at(k + 1)

            def body(r, _):
                done = attend(g, to * per_part + r, lags, False, True)
                obuf[g, to, pl.ds(pl.multiple_of(r * TILE, TILE), TILE), :] = done
                return 0
            lax.fori_loop(0, per_part, body, 0)

            @pl.when(k < nh - 1)
            def _():
                give(g, to).start()
            return 0
        lax.fori_loop(0, nh, chunk, 0)

    for g in range(groups):
        sweep(g, (0,), True)

    def forward(g, lag):
        arrive(g, lag)
        if lag == 2:
            along(g, 2).start()
        else:
            on_core(1, across(g).start)
        beside(g, lag).start()

    forward(0, 2)
    arrive(0, 1)
    sweep(0, (1, 2), False)
    forward(0, 4)
    forward(1, 2)
    arrive(0, 3)
    arrive(0, 5)
    finish(0, (3, 4, 5))
    arrive(1, 1)
    sweep(1, (1, 2), False)
    forward(1, 4)
    arrive(1, 3)
    arrive(1, 5)
    finish(1, (3, 4, 5))

    for by in range(1, nh):
        frm = head_at(by)
        for g in range(groups):
            slot = rbuf.at[g, frm]
            pltpu.make_async_remote_copy(
                src_ref=slot, dst_ref=slot, send_sem=as_sem.at[g, frm], recv_sem=ar_sem.at[g, frm],
                device_id=(me, frm), device_id_type=MESH).wait_recv()

    def place(ref_of, frm):
        halves = [ref_of(g)[...].astype(jnp.float32).reshape(part, per, width) for g in range(groups)]
        out_ref[:, pl.ds(pl.multiple_of(frm * heads, heads), heads), :] = jnp.concatenate(halves, axis=1).astype(jnp.bfloat16)

    for by in range(1, nh):
        frm = head_at(by)
        place(lambda g: rbuf.at[g, frm], frm)
    place(lambda g: obuf.at[g, mh], mh)

    for g in range(groups):
        for lag in (0, 2):
            along(g, lag).wait_send()
        on_core(1, across(g).wait_send)
        on_core(0, beside(g, 0).wait_send)
        beside(g, 2).wait_send()
        beside(g, 4).wait_send()
        for by in range(1, nh):
            give(g, head_at(by)).wait_send()


def local(nc, nh, queries, keys, values, doc_lengths):
    rows, heads, width = queries.shape
    groups = keys.shape[1]
    per = heads // groups
    part = rows // nh
    kv = jnp.transpose(jnp.stack((keys, values)), (2, 0, 1, 3))
    bf, f32 = jnp.bfloat16, jnp.float32
    vmem = pl.BlockSpec(memory_space=pltpu.VMEM)
    return pl.pallas_call(
        functools.partial(kernel, nc, nh),
        out_shape=jax.ShapeDtypeStruct((part, heads * nh, width), bf),
        in_specs=[pl.BlockSpec(memory_space=pltpu.SMEM), vmem, vmem],
        out_specs=vmem,
        scratch_shapes=[
            pltpu.VMEM((groups, rows * per, 2 * width), bf),
            pltpu.VMEM((LAGS, rows, LANES), bf),
            pltpu.VMEM((groups, LAGS - 1, 2, rows, width), bf),
            pltpu.VMEM((groups, rows * per, 2 * width), f32),
            pltpu.VMEM((groups, rows * per, LANES), f32),
            pltpu.VMEM((groups, nh, part * per, width), bf),
            pltpu.VMEM((groups, nh, part * per, width), bf),
            pltpu.SemaphoreType.DMA((groups, 3)),
            pltpu.SemaphoreType.DMA((groups, 3)),
            pltpu.SemaphoreType.DMA((groups, LAGS - 1)),
            pltpu.SemaphoreType.DMA((groups, nh)),
            pltpu.SemaphoreType.DMA((groups, nh)),
        ],
        compiler_params=pltpu.CompilerParams(
            collective_id=0, has_side_effects=True, vmem_limit_bytes=48 * 2**20),
        name="attend",
    )(doc_lengths, queries, kv)


def solution(mesh):
    nc, nh = mesh.shape["ctx"], mesh.shape["head"]
    in_specs = (P("ctx", "head", None), P("ctx", "head", None), P("ctx", "head", None), P())
    out_specs = P(("ctx", "head"), None, None)
    return jax.shard_map(
        functools.partial(local, nc, nh), mesh=mesh, in_specs=in_specs, out_specs=out_specs, check_vma=False)
```

time: 81.8 us -> 52.1 us (0.64)
  the two profiles are of different devices: /device:TPU:24 before, /device:TPU:6 now
where the time goes in v1:
time: 52.1 us; the launch traced here: 52 us
  Pallas kernels  49.2 us (94%)
  local copies, waits for them, and re-layouts  2.74 us (5%)
    pallas_call x1, Pallas kernels, local(): pl.pallas_call(functools.partial(kernel, nc, nh), out_shape=jax.ShapeDtyp...  49.2 us
    unnamed x5, local copies, waits for them, and re-layouts  1.65 us
    another operation x1, local copies, waits for them, and re-layouts, local(): kv = jnp.transpose(jnp.stack((keys, values)), (2, 0, 1, 3))  1.09 us

profile of v1, /device:TPU:6, one launch (start us, length us, event | category | flops | bytes accessed | tf_op | source)
XLA Modules:
  0.0 52.0 jit_solution(3218425814008855310)
XLA Ops:
  0.0 0.0 copy-start
  0.0 1.1 %copy_bitcast_fusion = (bf16[1,256,2,128]{3,1,0,2:T(8,128)(2,1)S(1)}, bf16[1,256,2,128]{3,1,0,2:T(8,128)(2,1)S(1)}) fusion(bf16[256,2,128]{2,1,0:T(2,128)(2,1)} %param.6, bf16[256,2,128]{2,1,0:T(2,128)(2,1)} %param.5), kind=kLoop, calls=%fused_computation.1 | loop fusion | bytes 524288 | tf_op jit(solution)/shard_map/stack | solution.py:253
  1.1 0.0 copy-start.1
  1.1 0.2 copy-done
  1.4 0.5 copy-done.1
  1.8 49.2 %attend.1 = bf16[64,64,128]{2,1,0:T(8,128)(2,1)S(1)} custom-call(s32[32]{0:T(128)S(1)} %copy-done.1, bf16[256,16,128]{2,1,0:T(8,128)(2,1)S(1)} %copy-done, bf16[2,2,256,128]{3,2,1,0:T(8,128)(2,1)S(1)} %maximum_bitcast_fusion.kv_ref), custom_call_target="tpu_custom_call" | custom-call | tf_op jit(solution)/shard_map/attend/pallas_call | solution.py:256
  51.0 1.0 %copy.10 = bf16[64,64,128]{2,1,0:T(8,128)(2,1)} copy(bf16[64,64,128]{2,1,0:T(8,128)(2,1)S(1)} %attend.1) | data formatting | bytes 2097152
  (1 shorter events, 0.0 us)
Async XLA Ops:
  0.0 1.4 %copy-start = (bf16[256,16,128]{2,1,0:T(8,128)(2,1)S(1)}, bf16[256,16,128]{2,1,0:T(8,128)(2,1)}, u32[]{:S(2)}) copy-start(bf16[256,16,128]{2,1,0:T(8,128)(2,1)} %q_ref.1) | copy-start | bytes 3145732
  1.1 0.7 %copy-start.1 = (s32[32]{0:T(128)S(1)}, s32[32]{0:T(128)}, u32[]{:S(2)}) copy-start(s32[32]{0:T(128)} %dl_ref.1) | copy-start | bytes 388

commit v2 on v1

v2 whole, which is shorter than its diff:
```python
import functools
import math

import jax
import jax.numpy as jnp
from jax import lax
from jax.experimental import pallas as pl
from jax.experimental.pallas import tpu as pltpu
from jax.sharding import PartitionSpec as P

MESH = pl.DeviceIdType.MESH
LAGS = 6
LANES = 128
MASKED = -1e30
TILE = 512


def kernel(
    nc, nh, dl_hbm, q_hbm, k_hbm, v_hbm, out_ref,
    dl_ref, q_ref, k_ref, v_ref, own, qe, msk, kvb, sbuf, acc, mst, obuf, rbuf,
    in_sem, zs_sem, ss_sem, kr_sem, as_sem, ar_sem,
):
    rows, heads, width = q_ref.shape
    groups = own.shape[0]
    per = heads // groups
    docs = dl_ref.shape[0]
    part = rows // nh
    tokens = TILE // per
    tiles = rows * per // TILE
    scale = math.log2(math.e) / math.sqrt(width)
    me = lax.axis_index("ctx")
    mh = lax.axis_index("head")
    core = lax.rem(me, 2)
    sib = me + 1 - 2 * core

    def head_at(by):
        return lax.rem(mh + by, nh)

    fetch = [
        pltpu.make_async_copy(src, dst, in_sem.at[n])
        for n, (src, dst) in enumerate(((k_hbm, k_ref), (v_hbm, v_ref), (q_hbm, q_ref), (dl_hbm, dl_ref)))
    ]
    for copy in fetch:
        copy.start()

    barrier = pltpu.get_barrier_semaphore()

    def greet(dev):
        pl.semaphore_signal(barrier, inc=1, device_id=dev, device_id_type=MESH)

    has_next = me + 2 < nc
    crosses = (core == 1) & (me >= 4) & (me + 1 < nc)

    @pl.when(me >= 2)
    def _():
        greet((me - 2, mh))

    @pl.when((core == 0) & (me >= 5))
    def _():
        greet((me - 1, mh))

    greet((sib, mh))
    for by in range(1, nh):
        greet((me, head_at(by)))

    def source(g, lag):
        return own.at[g] if lag == 0 else kvb.at[g, lag - 1]

    def along(g, lag, p):
        return pltpu.make_async_remote_copy(
            src_ref=source(g, lag).at[p], dst_ref=kvb.at[g, lag + 1, p],
            send_sem=zs_sem.at[g, lag // 2, p], recv_sem=kr_sem.at[g, lag + 1, p],
            device_id=(me + 2, mh), device_id_type=MESH)

    def across(g, p):
        return pltpu.make_async_remote_copy(
            src_ref=kvb.at[g, 3, p], dst_ref=kvb.at[g, 4, p],
            send_sem=zs_sem.at[g, 2, p], recv_sem=kr_sem.at[g, 4, p],
            device_id=(me + 1, mh), device_id_type=MESH)

    def beside(g, lag, p):
        there = lag - 2 * core
        return pltpu.make_async_remote_copy(
            src_ref=source(g, lag).at[p], dst_ref=kvb.at[g, there, p],
            send_sem=ss_sem.at[g, lag // 2, p], recv_sem=kr_sem.at[g, there, p],
            device_id=(sib, mh), device_id_type=MESH)

    def arrive(g, lag, p):
        slot = kvb.at[g, lag - 1, p]
        pltpu.make_async_remote_copy(
            src_ref=slot, dst_ref=slot, send_sem=zs_sem.at[g, 0, p], recv_sem=kr_sem.at[g, lag - 1, p],
            device_id=(sib, mh), device_id_type=MESH).wait_recv()

    def send_own(g, p):
        @pl.when(has_next)
        def _():
            along(g, 0, p).start()

        @pl.when(core == 0)
        def _():
            beside(g, 0, p).start()

    def forward(g, lag, p):
        @pl.when(me >= lag)
        def _():
            arrive(g, lag, p)
            if lag == 2:
                @pl.when(has_next)
                def _():
                    along(g, 2, p).start()
            else:
                @pl.when(crosses)
                def _():
                    across(g, p).start()
            beside(g, lag, p).start()

    def await_lag(g, lag):
        @pl.when(me >= lag)
        def _():
            for p in range(2):
                arrive(g, lag, p)

    fetch[3].wait()

    lane = lax.broadcasted_iota(jnp.int32, (8, LANES), 1)
    starts = jnp.full((8, LANES), 1 << 30, jnp.int32)
    ends = jnp.zeros((8, LANES), jnp.int32)
    total = jnp.int32(0)
    for d in range(docs):
        upto = total + dl_ref[d]
        starts = jnp.where(lane == d, total, starts)
        ends = jnp.where(lane == d, upto, ends)
        total = upto
    starts, ends = starts[0:1], ends[0:1]

    pick_row = lax.broadcasted_iota(jnp.int32, (groups * LANES, groups * LANES), 0)
    pick_col = lax.broadcasted_iota(jnp.int32, (groups * LANES, groups * LANES), 1)
    pick = jnp.where(pick_col == lax.rem(pick_row, LANES) * groups + pick_row // LANES, 1.0, 0.0).astype(jnp.bfloat16)
    fetch[0].wait()
    fetch[1].wait()
    for c in range(rows // LANES):
        at_row = c * LANES
        both = [
            jnp.dot(pick, ref[c * groups * LANES:(c + 1) * groups * LANES, :], preferred_element_type=jnp.float32)
            for ref in (k_ref, v_ref)
        ]
        for g in range(groups):
            own[g, 0, at_row:at_row + LANES, :] = both[0][g * LANES:(g + 1) * LANES].astype(jnp.bfloat16)
            own[g, 1, at_row:at_row + LANES, :] = jnp.transpose(both[1][g * LANES:(g + 1) * LANES]).astype(jnp.bfloat16)

    for lag in range(LAGS):
        pos = (me - lag) * rows + lax.broadcasted_iota(jnp.int32, (rows, LANES), 0)
        inside = (pos >= starts) & (pos < ends)
        msk[lag] = jnp.where(inside, 0.0, MASKED).astype(jnp.bfloat16)

    for lag in range(1, LAGS):
        @pl.when(me < lag)
        def _():
            kvb[:, lag - 1] = jnp.zeros((groups, 2, rows, width), jnp.bfloat16)

    pl.semaphore_wait(barrier, nh + has_next.astype(jnp.int32) + crosses.astype(jnp.int32))

    for p in range(2):
        send_own(0, p)

    fetch[2].wait()

    def gather_queries(r, _):
        first = pl.multiple_of(r * tokens, tokens)
        at_row = pl.multiple_of(r * TILE, TILE)
        x = q_ref[pl.ds(first, tokens)].astype(jnp.float32)
        pos = me * rows + first + lax.broadcasted_iota(jnp.int32, (tokens, per, LANES), 0)
        inside = (pos >= starts[None]) & (pos < ends[None])
        hot = jnp.where(inside, 1.0, 0.0).reshape(TILE, LANES).astype(jnp.bfloat16)
        for g in range(groups):
            qg = x[:, g * per:(g + 1) * per, :].reshape(TILE, width).astype(jnp.bfloat16)
            qe[g, pl.ds(at_row, TILE), 0:width] = qg
            qe[g, pl.ds(at_row, TILE), width:2 * width] = hot
        return 0

    lax.fori_loop(0, tiles, gather_queries, 0)

    ones = jnp.ones((16, rows), jnp.bfloat16)

    def score(g, r, lags, slot):
        q = qe[g, pl.ds(pl.multiple_of(r * TILE, TILE), TILE), :]
        top = None
        for n, lag in enumerate(lags):
            k = jnp.concatenate([source(g, lag)[0], msk[lag]], axis=1)
            s = lax.dot_general(k, q, (((1,), (1,)), ((), ())), preferred_element_type=jnp.float32)
            if lag == 0:
                key = lax.broadcasted_iota(jnp.int32, (rows, TILE), 0)
                tok = r * tokens + lax.broadcasted_iota(jnp.int32, (rows, TILE), 1) // per
                s = jnp.where(key <= tok, s, MASKED)
            sbuf[slot, n] = s
            high = jnp.max(s, axis=0, keepdims=True)
            top = high if top is None else jnp.maximum(top, high)
        return top

    def weigh(g, r, lags, slot, top, first, last):
        if not first:
            before = mst[g, r, 0:1, :]
            top = jnp.maximum(before, top)
        low = top * scale
        mixed = None
        for n, lag in enumerate(lags):
            w = jnp.exp2(sbuf[slot, n] * scale - low).astype(jnp.bfloat16)
            vt = source(g, lag)[1]
            vt = jnp.concatenate([vt[:LANES], vt[LANES:]], axis=1)
            vt = jnp.concatenate([vt, ones], axis=0)
            out = jnp.dot(vt, w, preferred_element_type=jnp.float32)
            mixed = out if mixed is None else mixed + out
        if not first:
            fade = jnp.exp2(before * scale - low)
            mixed = mixed + acc[g, r] * fade
        if not last:
            mst[g, r] = jnp.broadcast_to(top, (8, TILE))
            acc[g, r] = mixed
            return None
        return jnp.transpose(mixed[:width] * (1.0 / mixed[width:width + 1])).astype(jnp.bfloat16)

    def sweep(g, lags, order, first, emit=None):
        top = score(g, order[0], lags, 0)
        for t, r in enumerate(order):
            if t + 1 < len(order):
                following = score(g, order[t + 1], lags, (t + 1) % 2)
            done = weigh(g, r, lags, t % 2, top, first, emit is not None)
            if emit is not None:
                emit(t, done)
            top = following

    def give(g, to):
        return pltpu.make_async_remote_copy(
            src_ref=obuf.at[g, to], dst_ref=rbuf.at[g, mh],
            send_sem=as_sem.at[g, to], recv_sem=ar_sem.at[g, mh],
            device_id=(me, to), device_id_type=MESH)

    everywhere = list(range(tiles))
    dests = [head_at(by) for by in (2, 1, 3, 0)]

    def first_sweep(g, _):
        sweep(g, (0,), everywhere, True)
        return 0

    lax.fori_loop(0, groups, first_sweep, 0)
    forward(0, 2, 0)

    def rest(g, _):
        def emit(t, done):
            obuf[g, dests[t]] = done
            if t < nh - 1:
                give(g, dests[t]).start()

        forward(g, 2, 1)

        @pl.when(g == 0)
        def _():
            send_own(1, 0)

            @pl.when(core == 0)
            def _():
                send_own(1, 1)

        await_lag(g, 1)
        sweep(g, (1, 2), everywhere, False)
        forward(g, 4, 0)
        forward(g, 4, 1)

        @pl.when((g == 0) & (core == 1))
        def _():
            send_own(1, 1)

        await_lag(g, 3)
        sweep(g, (3, 4), everywhere, False)

        @pl.when(g == 0)
        def _():
            forward(1, 2, 0)

        await_lag(g, 5)
        sweep(g, (5,), dests, False, emit)
        return 0

    lax.fori_loop(0, groups, rest, 0)

    def place(refs, frm):
        halves = [ref[...].astype(jnp.float32).reshape(part, per, width) for ref in refs]
        out_ref[:, pl.ds(pl.multiple_of(frm * heads, heads), heads), :] = jnp.concatenate(halves, axis=1).astype(jnp.bfloat16)

    place([obuf.at[g, mh] for g in range(groups)], mh)
    for by in (3, 1, 2):
        frm = head_at(by)
        for g in range(groups):
            slot = rbuf.at[g, frm]
            pltpu.make_async_remote_copy(
                src_ref=slot, dst_ref=slot, send_sem=as_sem.at[g, frm], recv_sem=ar_sem.at[g, frm],
                device_id=(me, frm), device_id_type=MESH).wait_recv()
        place([rbuf.at[g, frm] for g in range(groups)], frm)

    def settle(g, _):
        for p in range(2):
            @pl.when(has_next)
            def _():
                along(g, 0, p).wait_send()

            @pl.when(has_next & (me >= 2))
            def _():
                along(g, 2, p).wait_send()

            @pl.when(crosses)
            def _():
                across(g, p).wait_send()

            @pl.when(core == 0)
            def _():
                beside(g, 0, p).wait_send()

            for lag in (2, 4):
                @pl.when(me >= lag)
                def _():
                    beside(g, lag, p).wait_send()
        for by in range(1, nh):
            give(g, head_at(by)).wait_send()
        return 0

    lax.fori_loop(0, groups, settle, 0)


def local(nc, nh, queries, keys, values, doc_lengths):
    rows, heads, width = queries.shape
    groups = keys.shape[1]
    per = heads // groups
    part = rows // nh
    tiles = rows * per // TILE
    bf, f32 = jnp.bfloat16, jnp.float32
    anywhere = pl.BlockSpec(memory_space=pl.ANY)
    return pl.pallas_call(
        functools.partial(kernel, nc, nh),
        out_shape=jax.ShapeDtypeStruct((part, heads * nh, width), bf),
        in_specs=[anywhere, anywhere, anywhere, anywhere],
        out_specs=pl.BlockSpec(memory_space=pltpu.VMEM),
        scratch_shapes=[
            pltpu.SMEM(doc_lengths.shape, jnp.int32),
            pltpu.VMEM((rows, heads, width), bf),
            pltpu.VMEM((rows * groups, width), bf),
            pltpu.VMEM((rows * groups, width), bf),
            pltpu.VMEM((groups, 2, rows, width), bf),
            pltpu.VMEM((groups, rows * per, 2 * width), bf),
            pltpu.VMEM((LAGS, rows, LANES), bf),
            pltpu.VMEM((groups, LAGS - 1, 2, rows, width), bf),
            pltpu.VMEM((2, 2, rows, TILE), f32),
            pltpu.VMEM((groups, tiles, width + 16, TILE), f32),
            pltpu.VMEM((groups, tiles, 8, TILE), f32),
            pltpu.VMEM((groups, nh, part * per, width), bf),
            pltpu.VMEM((groups, nh, part * per, width), bf),
            pltpu.SemaphoreType.DMA((4,)),
            pltpu.SemaphoreType.DMA((groups, 3, 2)),
            pltpu.SemaphoreType.DMA((groups, 3, 2)),
            pltpu.SemaphoreType.DMA((groups, LAGS - 1, 2)),
            pltpu.SemaphoreType.DMA((groups, nh)),
            pltpu.SemaphoreType.DMA((groups, nh)),
        ],
        compiler_params=pltpu.CompilerParams(
            collective_id=0, has_side_effects=True, vmem_limit_bytes=56 * 2**20),
        name="attend",
    )(doc_lengths, queries, keys.reshape(rows * groups, width), values.reshape(rows * groups, width))


def solution(mesh):
    nc, nh = mesh.shape["ctx"], mesh.shape["head"]
    in_specs = (P("ctx", "head", None), P("ctx", "head", None), P("ctx", "head", None), P())
    out_specs = P(("ctx", "head"), None, None)
    return jax.shard_map(
        functools.partial(local, nc, nh), mesh=mesh, in_specs=in_specs, out_specs=out_specs, check_vma=False)
```

time: 52.1 us -> 38.1 us (0.73)
  the two profiles are of different devices: /device:TPU:6 before, /device:TPU:24 now
where the time goes in v2:
time: 38.1 us; the launch traced here: 37.8 us
  Pallas kernels  35.6 us (93%)
  local copies, waits for them, and re-layouts  2.26 us (6%)
    pallas_call x1, Pallas kernels, local(): pl.pallas_call(functools.partial(kernel, nc, nh), out_shape=jax.ShapeDtyp...  35.6 us
    unnamed x1, local copies, waits for them, and re-layouts  2.26 us

profile of v2, /device:TPU:24, one launch (start us, length us, event | category | flops | bytes accessed | tf_op | source)
XLA Modules:
  0.0 37.8 jit_solution(14214500350216265357)
XLA Ops:
  0.0 35.6 %attend.1 = bf16[64,64,128]{2,1,0:T(8,128)(2,1)} custom-call(s32[32]{0:T(128)} %dl_hbm.1, bf16[256,16,128]{2,1,0:T(8,128)(2,1)} %q_hbm.1, bf16[512,128]{1,0:T(8,128)(2,1)} %bitcast.2, bf16[512,128]{1,0:T(8,128)(2,1)} %bitcast.3), custom_call_target="tpu_custom_call" | custom-call | tf_op jit(solution)/shard_map/attend/pallas_call | solution.py:337
  35.6 2.3 %copy.6 = bf16[64,64,128]{2,1,0:T(8,128)(2,1)} copy(bf16[64,64,128]{2,1,0:T(8,128)(2,1)} %attend.1) | data formatting | bytes 2097152

commit v3 on v2

--- a/solution.py
+++ b/solution.py
@@ -13,12 +13,13 @@
 LANES = 128
 MASKED = -1e30
 TILE = 512
+DEEP = 8
 
 
 def kernel(
     nc, nh, dl_hbm, q_hbm, k_hbm, v_hbm, out_ref,
-    dl_ref, q_ref, k_ref, v_ref, own, qe, msk, kvb, sbuf, acc, mst, obuf, rbuf,
-    in_sem, zs_sem, ss_sem, kr_sem, as_sem, ar_sem,
+    dl_ref, q_ref, k_ref, v_ref, own, qe, msk, kvb, sbuf, acc, mst, obuf, rbuf, relay,
+    in_sem, re_sem, zs_sem, ss_sem, kr_sem, as_sem, ar_sem,
 ):
     rows, heads, width = q_ref.shape
     groups = own.shape[0]
@@ -51,6 +52,15 @@
     has_next = me + 2 < nc
     crosses = (core == 1) & (me >= 4) & (me + 1 < nc)
 
+    z = lax.rem(me // 2, DEEP)
+    row_first, row_last = me < 2 * DEEP, me >= nc - 2 * DEEP
+    last_chip = (z == DEEP - 1) & jnp.logical_not(row_last)
+    lends = ((z == DEEP - 2) | ((z == DEEP - 3) & (core == 1))) & jnp.logical_not(row_last)
+    hands = ((z == 3) | ((z == 2) & (core == 1))) & jnp.logical_not(row_first)
+    to_hands = 10
+    hand_on = jnp.where(z == 3, me - 6, me - 5)
+    handed = groups - 1
+
     @pl.when(me >= 2)
     def _():
         greet((me - 2, mh))
@@ -58,6 +68,18 @@
     @pl.when((core == 0) & (me >= 5))
     def _():
         greet((me - 1, mh))
+
+    @pl.when(hands)
+    def _():
+        greet((me - to_hands, mh))
+
+    @pl.when((z == 0) & jnp.logical_not(row_first))
+    def _():
+        greet((me + 6, mh))
+
+        @pl.when(core == 0)
+        def _():
+            greet((me + 5, mh))
 
     greet((sib, mh))
     for by in range(1, nh):
@@ -84,6 +106,23 @@
             src_ref=source(g, lag).at[p], dst_ref=kvb.at[g, there, p],
             send_sem=ss_sem.at[g, lag // 2, p], recv_sem=kr_sem.at[g, there, p],
             device_id=(sib, mh), device_id_type=MESH)
+
+    def lend(p):
+        return pltpu.make_async_remote_copy(
+            src_ref=own.at[handed, p], dst_ref=relay.at[p], send_sem=re_sem.at[0, p], recv_sem=re_sem.at[1, p],
+            device_id=(me + to_hands, mh), device_id_type=MESH)
+
+    def hand(p):
+        slot = jnp.where(z == 3, 3, 4)
+        return pltpu.make_async_remote_copy(
+            src_ref=relay.at[p], dst_ref=kvb.at[handed, slot, p],
+            send_sem=re_sem.at[2, p], recv_sem=kr_sem.at[handed, slot, p],
+            device_id=(hand_on, mh), device_id_type=MESH)
+
+    def relayed(p):
+        pltpu.make_async_remote_copy(
+            src_ref=relay.at[p], dst_ref=relay.at[p], send_sem=re_sem.at[0, p], recv_sem=re_sem.at[1, p],
+            device_id=(sib, mh), device_id_type=MESH).wait_recv()
 
     def arrive(g, lag, p):
         slot = kvb.at[g, lag - 1, p]
@@ -105,11 +144,11 @@
         def _():
             arrive(g, lag, p)
             if lag == 2:
-                @pl.when(has_next)
+                @pl.when(has_next & jnp.logical_not(last_chip & (g == handed)))
                 def _():
                     along(g, 2, p).start()
             else:
-                @pl.when(crosses)
+                @pl.when(crosses & jnp.logical_not(last_chip & (g == handed)))
                 def _():
                     across(g, p).start()
             beside(g, lag, p).start()
@@ -123,13 +162,18 @@
     fetch[3].wait()
 
     lane = lax.broadcasted_iota(jnp.int32, (8, LANES), 1)
+    down = lax.broadcasted_iota(jnp.int32, (docs, LANES), 0)
     starts = jnp.full((8, LANES), 1 << 30, jnp.int32)
     ends = jnp.zeros((8, LANES), jnp.int32)
+    down_from = jnp.zeros((docs, LANES), jnp.int32)
+    down_to = down_from
     total = jnp.int32(0)
     for d in range(docs):
         upto = total + dl_ref[d]
         starts = jnp.where(lane == d, total, starts)
         ends = jnp.where(lane == d, upto, ends)
+        down_from = jnp.where(down == d, total, down_from)
+        down_to = jnp.where(down == d, upto, down_to)
         total = upto
     starts, ends = starts[0:1], ends[0:1]
 
@@ -158,24 +202,40 @@
         def _():
             kvb[:, lag - 1] = jnp.zeros((groups, 2, rows, width), jnp.bfloat16)
 
-    pl.semaphore_wait(barrier, nh + has_next.astype(jnp.int32) + crosses.astype(jnp.int32))
+    pl.semaphore_wait(barrier, nh + sum(c.astype(jnp.int32) for c in (has_next, crosses, lends, hands)))
 
     for p in range(2):
         send_own(0, p)
 
+    @pl.when(lends)
+    def _():
+        for p in range(2):
+            lend(p).start()
+
+    @pl.when(z == 0)
+    def _():
+        for p in range(2):
+            send_own(1, p)
+
     fetch[2].wait()
+
+    eye_row = lax.broadcasted_iota(jnp.int32, (width, width), 0)
+    eye_col = lax.broadcasted_iota(jnp.int32, (width, width), 1)
+    eye = jnp.where(eye_row == eye_col, 1.0, 0.0).astype(jnp.bfloat16)
+    wide = lambda x: jnp.concatenate([x] * (TILE // LANES), axis=1)
+    doc_from, doc_to = wide(down_from), wide(down_to)
 
     def gather_queries(r, _):
         first = pl.multiple_of(r * tokens, tokens)
-        at_row = pl.multiple_of(r * TILE, TILE)
         x = q_ref[pl.ds(first, tokens)].astype(jnp.float32)
-        pos = me * rows + first + lax.broadcasted_iota(jnp.int32, (tokens, per, LANES), 0)
-        inside = (pos >= starts[None]) & (pos < ends[None])
-        hot = jnp.where(inside, 1.0, 0.0).reshape(TILE, LANES).astype(jnp.bfloat16)
+        pos = me * rows + first + lax.broadcasted_iota(jnp.int32, (docs, TILE), 1) // per
+        hot = jnp.where((pos >= doc_from) & (pos < doc_to), 1.0, 0.0).astype(jnp.bfloat16)
         for g in range(groups):
             qg = x[:, g * per:(g + 1) * per, :].reshape(TILE, width).astype(jnp.bfloat16)
-            qe[g, pl.ds(at_row, TILE), 0:width] = qg
-            qe[g, pl.ds(at_row, TILE), width:2 * width] = hot
+            turned = lax.dot_general(eye, qg, (((1,), (1,)), ((), ())), preferred_element_type=jnp.float32)
+            qe[g, r, 0:width] = turned.astype(jnp.bfloat16)
+            qe[g, r, width:width + docs] = hot
+            qe[g, r, width + docs:2 * width] = jnp.zeros((width - docs, TILE), jnp.bfloat16)
         return 0
 
     lax.fori_loop(0, tiles, gather_queries, 0)
@@ -183,50 +243,41 @@
     ones = jnp.ones((16, rows), jnp.bfloat16)
 
     def score(g, r, lags, slot):
-        q = qe[g, pl.ds(pl.multiple_of(r * TILE, TILE), TILE), :]
-        top = None
-        for n, lag in enumerate(lags):
-            k = jnp.concatenate([source(g, lag)[0], msk[lag]], axis=1)
-            s = lax.dot_general(k, q, (((1,), (1,)), ((), ())), preferred_element_type=jnp.float32)
-            if lag == 0:
-                key = lax.broadcasted_iota(jnp.int32, (rows, TILE), 0)
-                tok = r * tokens + lax.broadcasted_iota(jnp.int32, (rows, TILE), 1) // per
-                s = jnp.where(key <= tok, s, MASKED)
-            sbuf[slot, n] = s
-            high = jnp.max(s, axis=0, keepdims=True)
-            top = high if top is None else jnp.maximum(top, high)
-        return top
-
-    def weigh(g, r, lags, slot, top, first, last):
-        if not first:
-            before = mst[g, r, 0:1, :]
-            top = jnp.maximum(before, top)
-        low = top * scale
-        mixed = None
-        for n, lag in enumerate(lags):
-            w = jnp.exp2(sbuf[slot, n] * scale - low).astype(jnp.bfloat16)
-            vt = source(g, lag)[1]
-            vt = jnp.concatenate([vt[:LANES], vt[LANES:]], axis=1)
-            vt = jnp.concatenate([vt, ones], axis=0)
-            out = jnp.dot(vt, w, preferred_element_type=jnp.float32)
-            mixed = out if mixed is None else mixed + out
-        if not first:
-            fade = jnp.exp2(before * scale - low)
-            mixed = mixed + acc[g, r] * fade
-        if not last:
-            mst[g, r] = jnp.broadcast_to(top, (8, TILE))
-            acc[g, r] = mixed
-            return None
-        return jnp.transpose(mixed[:width] * (1.0 / mixed[width:width + 1])).astype(jnp.bfloat16)
+        k = [jnp.concatenate([source(g, lag)[0], msk[lag]], axis=1) for lag in lags]
+        k = jnp.concatenate(k, axis=0)
+        s = jnp.dot(k, qe[g, r], preferred_element_type=jnp.float32)
+        if lags == (0,):
+            key = lax.broadcasted_iota(jnp.int32, (rows, TILE), 0)
+            tok = r * tokens + lax.broadcasted_iota(jnp.int32, (rows, TILE), 1) // per
+            s = jnp.where(key <= tok, s, MASKED)
+        sbuf[slot, 0:len(lags) * rows] = s
+        return jnp.max(s, axis=0, keepdims=True)
+
+    def weigh(g, lags, slot, low):
+        w = jnp.exp2(sbuf[slot, 0:len(lags) * rows] * scale - low).astype(jnp.bfloat16)
+        vt = []
+        for lag in lags:
+            half = source(g, lag)[1]
+            vt.append(jnp.concatenate([jnp.concatenate([half[:LANES], half[LANES:]], axis=1), ones], axis=0))
+        return jnp.dot(jnp.concatenate(vt, axis=1), w, preferred_element_type=jnp.float32)
 
     def sweep(g, lags, order, first, emit=None):
         top = score(g, order[0], lags, 0)
         for t, r in enumerate(order):
+            if not first:
+                before = mst[g, r, 0:1, :]
+                top = jnp.maximum(before, top)
+            low = top * scale
             if t + 1 < len(order):
                 following = score(g, order[t + 1], lags, (t + 1) % 2)
-            done = weigh(g, r, lags, t % 2, top, first, emit is not None)
-            if emit is not None:
-                emit(t, done)
+            mixed = weigh(g, lags, t % 2, low)
+            if not first:
+                mixed = mixed + acc[g, r] * jnp.exp2(before * scale - low)
+            if emit is None:
+                mst[g, r] = jnp.broadcast_to(top, (8, TILE))
+                acc[g, r] = mixed
+            else:
+                emit(t, jnp.transpose(mixed[:width] * (1.0 / mixed[width:width + 1])).astype(jnp.bfloat16))
             top = following
 
     def give(g, to):
@@ -253,7 +304,7 @@
 
         forward(g, 2, 1)
 
-        @pl.when(g == 0)
+        @pl.when((g == 0) & (z > 0))
         def _():
             send_own(1, 0)
 
@@ -266,9 +317,17 @@
         forward(g, 4, 0)
         forward(g, 4, 1)
 
-        @pl.when((g == 0) & (core == 1))
-        def _():
-            send_own(1, 1)
+        @pl.when(g == 0)
+        def _():
+            @pl.when((core == 1) & (z > 0))
+            def _():
+                send_own(1, 1)
+
+            @pl.when(hands)
+            def _():
+                for p in range(2):
+                    relayed(p)
+                    hand(p).start()
 
         await_lag(g, 3)
         sweep(g, (3, 4), everywhere, False)
@@ -303,11 +362,11 @@
             def _():
                 along(g, 0, p).wait_send()
 
-            @pl.when(has_next & (me >= 2))
+            @pl.when(has_next & (me >= 2) & jnp.logical_not(last_chip & (g == handed)))
             def _():
                 along(g, 2, p).wait_send()
 
-            @pl.when(crosses)
+            @pl.when(crosses & jnp.logical_not(last_chip & (g == handed)))
             def _():
                 across(g, p).wait_send()
 
@@ -324,6 +383,15 @@
         return 0
 
     lax.fori_loop(0, groups, settle, 0)
+
+    for p in range(2):
+        @pl.when(lends)
+        def _():
+            lend(p).wait_send()
+
+        @pl.when(hands)
+        def _():
+            hand(p).wait_send()
 
 
 def local(nc, nh, queries, keys, values, doc_lengths):
@@ -336,7 +404,7 @@
     anywhere = pl.BlockSpec(memory_space=pl.ANY)
     return pl.pallas_call(
         functools.partial(kernel, nc, nh),
-        out_shape=jax.ShapeDtypeStruct((part, heads * nh, width), bf),
+        out_shape=pltpu.VMEM((part, heads * nh, width), bf),
         in_specs=[anywhere, anywhere, anywhere, anywhere],
         out_specs=pl.BlockSpec(memory_space=pltpu.VMEM),
         scratch_shapes=[
@@ -345,15 +413,17 @@
             pltpu.VMEM((rows * groups, width), bf),
             pltpu.VMEM((rows * groups, width), bf),
             pltpu.VMEM((groups, 2, rows, width), bf),
-            pltpu.VMEM((groups, rows * per, 2 * width), bf),
+            pltpu.VMEM((groups, tiles, 2 * width, TILE), bf),
             pltpu.VMEM((LAGS, rows, LANES), bf),
             pltpu.VMEM((groups, LAGS - 1, 2, rows, width), bf),
-            pltpu.VMEM((2, 2, rows, TILE), f32),
+            pltpu.VMEM((2, 2 * rows, TILE), f32),
             pltpu.VMEM((groups, tiles, width + 16, TILE), f32),
             pltpu.VMEM((groups, tiles, 8, TILE), f32),
             pltpu.VMEM((groups, nh, part * per, width), bf),
             pltpu.VMEM((groups, nh, part * per, width), bf),
+            pltpu.VMEM((2, rows, width), bf),
             pltpu.SemaphoreType.DMA((4,)),
+            pltpu.SemaphoreType.DMA((3, 2)),
             pltpu.SemaphoreType.DMA((groups, 3, 2)),
             pltpu.SemaphoreType.DMA((groups, 3, 2)),
             pltpu.SemaphoreType.DMA((groups, LAGS - 1, 2)),
@@ -361,7 +431,7 @@
             pltpu.SemaphoreType.DMA((groups, nh)),
         ],
         compiler_params=pltpu.CompilerParams(
-            collective_id=0, has_side_effects=True, vmem_limit_bytes=56 * 2**20),
+            collective_id=0, has_side_effects=True, vmem_limit_bytes=53 * 2**20),
         name="attend",
     )(doc_lengths, queries, keys.reshape(rows * groups, width), values.reshape(rows * groups, width))
 

time: 38.1 us -> 34.9 us (0.916)
  Pallas kernels: 35.6 us -> 33.4 us
  local copies, waits for them, and re-layouts: 2.26 us -> 0.97 us
    pallas_call x1, Pallas kernels: 35.6 us -> 33.4 us  [local(): pl.pallas_call(functools.partial(kernel, nc, nh), out_shape=pltpu.VMEM((p...]
    unnamed x1, local copies, waits for them, and re-layouts: 2.26 us -> 0.97 us
where the time goes in v3:
time: 34.9 us; the launch traced here: 34.4 us
  Pallas kernels  33.4 us (96%)
  local copies, waits for them, and re-layouts  0.97 us (3%)
    pallas_call x1, Pallas kernels, local(): pl.pallas_call(functools.partial(kernel, nc, nh), out_shape=pltpu.VMEM((p...  33.4 us
    unnamed x1, local copies, waits for them, and re-layouts  0.97 us

profile of v3, /device:TPU:24, one launch (start us, length us, event | category | flops | bytes accessed | tf_op | source)
XLA Modules:
  0.0 34.4 jit_solution(1938114983534390687)
XLA Ops:
  0.0 33.4 %attend.1 = bf16[64,64,128]{2,1,0:T(8,128)(2,1)S(1)} custom-call(s32[32]{0:T(128)} %dl_hbm.1, bf16[256,16,128]{2,1,0:T(8,128)(2,1)} %q_hbm.1, bf16[512,128]{1,0:T(8,128)(2,1)} %bitcast.2, bf16[512,128]{1,0:T(8,128)(2,1)} %bitcast.3), custom_call_target="tpu_custom_call" | custom-call | tf_op jit(solution)/shard_map/attend/pallas_call | solution.py:405
  33.5 1.0 %copy.6 = bf16[64,64,128]{2,1,0:T(8,128)(2,1)} copy(bf16[64,64,128]{2,1,0:T(8,128)(2,1)S(1)} %attend.1) | data formatting | bytes 2097152

commit v4 on v3

--- a/solution.py
+++ b/solution.py
@@ -55,10 +55,12 @@
     z = lax.rem(me // 2, DEEP)
     row_first, row_last = me < 2 * DEEP, me >= nc - 2 * DEEP
     last_chip = (z == DEEP - 1) & jnp.logical_not(row_last)
+    first_chip = (z == 0) & jnp.logical_not(row_first)
+    spared = last_chip | first_chip
     lends = ((z == DEEP - 2) | ((z == DEEP - 3) & (core == 1))) & jnp.logical_not(row_last)
-    hands = ((z == 3) | ((z == 2) & (core == 1))) & jnp.logical_not(row_first)
-    to_hands = 10
-    hand_on = jnp.where(z == 3, me - 6, me - 5)
+    hands_same = (z == 3) & jnp.logical_not(row_first)
+    hands_other = ((z == 2) | (z == 3)) & (core == 1) & jnp.logical_not(row_first)
+    hands = hands_same | hands_other
     handed = groups - 1
 
     @pl.when(me >= 2)
@@ -71,15 +73,15 @@
 
     @pl.when(hands)
     def _():
-        greet((me - to_hands, mh))
-
-    @pl.when((z == 0) & jnp.logical_not(row_first))
+        greet((me - 10, mh))
+
+    @pl.when(first_chip)
     def _():
         greet((me + 6, mh))
 
-        @pl.when(core == 0)
-        def _():
-            greet((me + 5, mh))
+    @pl.when((z <= 1) & (core == 0) & jnp.logical_not(row_first))
+    def _():
+        greet((me + 5, mh))
 
     greet((sib, mh))
     for by in range(1, nh):
@@ -110,14 +112,17 @@
     def lend(p):
         return pltpu.make_async_remote_copy(
             src_ref=own.at[handed, p], dst_ref=relay.at[p], send_sem=re_sem.at[0, p], recv_sem=re_sem.at[1, p],
-            device_id=(me + to_hands, mh), device_id_type=MESH)
-
-    def hand(p):
-        slot = jnp.where(z == 3, 3, 4)
-        return pltpu.make_async_remote_copy(
-            src_ref=relay.at[p], dst_ref=kvb.at[handed, slot, p],
-            send_sem=re_sem.at[2, p], recv_sem=kr_sem.at[handed, slot, p],
-            device_id=(hand_on, mh), device_id_type=MESH)
+            device_id=(me + 10, mh), device_id_type=MESH)
+
+    def hand_same(p):
+        return pltpu.make_async_remote_copy(
+            src_ref=relay.at[p], dst_ref=kvb.at[handed, 3, p], send_sem=re_sem.at[2, p], recv_sem=kr_sem.at[handed, 3, p],
+            device_id=(me - 6, mh), device_id_type=MESH)
+
+    def hand_other(p):
+        return pltpu.make_async_remote_copy(
+            src_ref=relay.at[p], dst_ref=kvb.at[handed, 4, p], send_sem=re_sem.at[3, p], recv_sem=kr_sem.at[handed, 4, p],
+            device_id=(me - 5, mh), device_id_type=MESH)
 
     def relayed(p):
         pltpu.make_async_remote_copy(
@@ -148,7 +153,7 @@
                 def _():
                     along(g, 2, p).start()
             else:
-                @pl.when(crosses & jnp.logical_not(last_chip & (g == handed)))
+                @pl.when(crosses & jnp.logical_not(spared & (g == handed)))
                 def _():
                     across(g, p).start()
             beside(g, lag, p).start()
@@ -158,6 +163,37 @@
         def _():
             for p in range(2):
                 arrive(g, lag, p)
+
+    pick_row = lax.broadcasted_iota(jnp.int32, (groups * LANES, groups * LANES), 0)
+    pick_col = lax.broadcasted_iota(jnp.int32, (groups * LANES, groups * LANES), 1)
+    pick = jnp.where(pick_col == lax.rem(pick_row, LANES) * groups + pick_row // LANES, 1.0, 0.0).astype(jnp.bfloat16)
+
+    def separate(ref, p):
+        for c in range(rows // LANES):
+            at_row = c * LANES
+            both = jnp.dot(pick, ref[c * groups * LANES:(c + 1) * groups * LANES, :], preferred_element_type=jnp.float32)
+            for g in range(groups):
+                one = both[g * LANES:(g + 1) * LANES]
+                own[g, p, at_row:at_row + LANES, :] = (jnp.transpose(one) if p else one).astype(jnp.bfloat16)
+
+    fetch[0].wait()
+    separate(k_ref, 0)
+    pl.semaphore_wait(barrier, nh + sum(c.astype(jnp.int32) for c in (has_next, crosses, lends, hands_same, hands_other)))
+
+    send_own(0, 0)
+    fetch[1].wait()
+    separate(v_ref, 1)
+    send_own(0, 1)
+
+    @pl.when(lends)
+    def _():
+        for p in range(2):
+            lend(p).start()
+
+    @pl.when(z == 0)
+    def _():
+        for p in range(2):
+            send_own(1, p)
 
     fetch[3].wait()
 
@@ -177,21 +213,6 @@
         total = upto
     starts, ends = starts[0:1], ends[0:1]
 
-    pick_row = lax.broadcasted_iota(jnp.int32, (groups * LANES, groups * LANES), 0)
-    pick_col = lax.broadcasted_iota(jnp.int32, (groups * LANES, groups * LANES), 1)
-    pick = jnp.where(pick_col == lax.rem(pick_row, LANES) * groups + pick_row // LANES, 1.0, 0.0).astype(jnp.bfloat16)
-    fetch[0].wait()
-    fetch[1].wait()
-    for c in range(rows // LANES):
-        at_row = c * LANES
-        both = [
-            jnp.dot(pick, ref[c * groups * LANES:(c + 1) * groups * LANES, :], preferred_element_type=jnp.float32)
-            for ref in (k_ref, v_ref)
-        ]
-        for g in range(groups):
-            own[g, 0, at_row:at_row + LANES, :] = both[0][g * LANES:(g + 1) * LANES].astype(jnp.bfloat16)
-            own[g, 1, at_row:at_row + LANES, :] = jnp.transpose(both[1][g * LANES:(g + 1) * LANES]).astype(jnp.bfloat16)
-
     for lag in range(LAGS):
         pos = (me - lag) * rows + lax.broadcasted_iota(jnp.int32, (rows, LANES), 0)
         inside = (pos >= starts) & (pos < ends)
@@ -201,21 +222,6 @@
         @pl.when(me < lag)
         def _():
             kvb[:, lag - 1] = jnp.zeros((groups, 2, rows, width), jnp.bfloat16)
-
-    pl.semaphore_wait(barrier, nh + sum(c.astype(jnp.int32) for c in (has_next, crosses, lends, hands)))
-
-    for p in range(2):
-        send_own(0, p)
-
-    @pl.when(lends)
-    def _():
-        for p in range(2):
-            lend(p).start()
-
-    @pl.when(z == 0)
-    def _():
-        for p in range(2):
-            send_own(1, p)
 
     fetch[2].wait()
 
@@ -242,19 +248,26 @@
 
     ones = jnp.ones((16, rows), jnp.bfloat16)
 
+    def skip(r, lags):
+        return r * tokens if lags == (LAGS - 1,) else 0
+
     def score(g, r, lags, slot):
-        k = [jnp.concatenate([source(g, lag)[0], msk[lag]], axis=1) for lag in lags]
+        low = skip(r, lags)
+        k = [jnp.concatenate([source(g, lag)[0, low:], msk[lag, low:]], axis=1) for lag in lags]
         k = jnp.concatenate(k, axis=0)
         s = jnp.dot(k, qe[g, r], preferred_element_type=jnp.float32)
         if lags == (0,):
             key = lax.broadcasted_iota(jnp.int32, (rows, TILE), 0)
             tok = r * tokens + lax.broadcasted_iota(jnp.int32, (rows, TILE), 1) // per
             s = jnp.where(key <= tok, s, MASKED)
-        sbuf[slot, 0:len(lags) * rows] = s
+        sbuf[slot, low:len(lags) * rows] = s
         return jnp.max(s, axis=0, keepdims=True)
 
-    def weigh(g, lags, slot, low):
-        w = jnp.exp2(sbuf[slot, 0:len(lags) * rows] * scale - low).astype(jnp.bfloat16)
+    def weigh(g, r, lags, slot, low):
+        cut = skip(r, lags)
+        w = jnp.exp2(sbuf[slot, cut:len(lags) * rows] * scale - low).astype(jnp.bfloat16)
+        if cut:
+            w = jnp.concatenate([jnp.zeros((cut, TILE), jnp.bfloat16), w], axis=0)
         vt = []
         for lag in lags:
             half = source(g, lag)[1]
@@ -270,7 +283,7 @@
             low = top * scale
             if t + 1 < len(order):
                 following = score(g, order[t + 1], lags, (t + 1) % 2)
-            mixed = weigh(g, lags, t % 2, low)
+            mixed = weigh(g, r, lags, t % 2, low)
             if not first:
                 mixed = mixed + acc[g, r] * jnp.exp2(before * scale - low)
             if emit is None:
@@ -298,15 +311,21 @@
 
     def rest(g, _):
         def emit(t, done):
-            obuf[g, dests[t]] = done
-            if t < nh - 1:
-                give(g, dests[t]).start()
-
-        forward(g, 2, 1)
+            obuf[g, t] = done
+
+            @pl.when(mh != t)
+            def _():
+                give(g, t).start()
+
+        @pl.when((g == 0) | (core == 1) | (z == 0))
+        def _():
+            forward(g, 2, 1)
 
         @pl.when((g == 0) & (z > 0))
         def _():
-            send_own(1, 0)
+            @pl.when(jnp.logical_not(last_chip & (core == 1)))
+            def _():
+                send_own(1, 0)
 
             @pl.when(core == 0)
             def _():
@@ -319,6 +338,10 @@
 
         @pl.when(g == 0)
         def _():
+            @pl.when(last_chip & (core == 1))
+            def _():
+                send_own(1, 0)
+
             @pl.when((core == 1) & (z > 0))
             def _():
                 send_own(1, 1)
@@ -327,7 +350,15 @@
             def _():
                 for p in range(2):
                     relayed(p)
-                    hand(p).start()
+
+                    @pl.when(hands_same)
+                    def _():
+                        hand_same(p).start()
+
+                for p in range(2):
+                    @pl.when(hands_other)
+                    def _():
+                        hand_other(p).start()
 
         await_lag(g, 3)
         sweep(g, (3, 4), everywhere, False)
@@ -336,8 +367,12 @@
         def _():
             forward(1, 2, 0)
 
+            @pl.when((core == 0) & (z > 0))
+            def _():
+                forward(1, 2, 1)
+
         await_lag(g, 5)
-        sweep(g, (5,), dests, False, emit)
+        sweep(g, (5,), everywhere, False, emit)
         return 0
 
     lax.fori_loop(0, groups, rest, 0)
@@ -366,7 +401,7 @@
             def _():
                 along(g, 2, p).wait_send()
 
-            @pl.when(crosses & jnp.logical_not(last_chip & (g == handed)))
+            @pl.when(crosses & jnp.logical_not(spared & (g == handed)))
             def _():
                 across(g, p).wait_send()
 
@@ -389,9 +424,13 @@
         def _():
             lend(p).wait_send()
 
-        @pl.when(hands)
-        def _():
-            hand(p).wait_send()
+        @pl.when(hands_same)
+        def _():
+            hand_same(p).wait_send()
+
+        @pl.when(hands_other)
+        def _():
+            hand_other(p).wait_send()
 
 
 def local(nc, nh, queries, keys, values, doc_lengths):
@@ -423,7 +462,7 @@
             pltpu.VMEM((groups, nh, part * per, width), bf),
             pltpu.VMEM((2, rows, width), bf),
             pltpu.SemaphoreType.DMA((4,)),
-            pltpu.SemaphoreType.DMA((3, 2)),
+            pltpu.SemaphoreType.DMA((4, 2)),
             pltpu.SemaphoreType.DMA((groups, 3, 2)),
             pltpu.SemaphoreType.DMA((groups, 3, 2)),
             pltpu.SemaphoreType.DMA((groups, LAGS - 1, 2)),

time: 34.9 us -> 34.8 us (level)
  no operation moved by 1% of the time
where the time goes in v4:
time: 34.8 us; the launch traced here: 34.6 us
  Pallas kernels  33.7 us (97%)
  local copies, waits for them, and re-layouts  0.97 us (3%)
    pallas_call x1, Pallas kernels, local(): pl.pallas_call(functools.partial(kernel, nc, nh), out_shape=pltpu.VMEM((p...  33.7 us
    unnamed x1, local copies, waits for them, and re-layouts  0.97 us

profile of v4, /device:TPU:24, one launch (start us, length us, event | category | flops | bytes accessed | tf_op | source)
XLA Modules:
  0.0 34.6 jit_solution(12601454314482038279)
XLA Ops:
  0.0 33.7 %attend.1 = bf16[64,64,128]{2,1,0:T(8,128)(2,1)S(1)} custom-call(s32[32]{0:T(128)} %dl_hbm.1, bf16[256,16,128]{2,1,0:T(8,128)(2,1)} %q_hbm.1, bf16[512,128]{1,0:T(8,128)(2,1)} %bitcast.2, bf16[512,128]{1,0:T(8,128)(2,1)} %bitcast.3), custom_call_target="tpu_custom_call" | custom-call | tf_op jit(solution)/shard_map/attend/pallas_call | solution.py:444
  33.7 1.0 %copy.6 = bf16[64,64,128]{2,1,0:T(8,128)(2,1)} copy(bf16[64,64,128]{2,1,0:T(8,128)(2,1)S(1)} %attend.1) | data formatting | bytes 2097152

commit v5 on v4

--- a/solution.py
+++ b/solution.py
@@ -323,9 +323,7 @@
 
         @pl.when((g == 0) & (z > 0))
         def _():
-            @pl.when(jnp.logical_not(last_chip & (core == 1)))
-            def _():
-                send_own(1, 0)
+            send_own(1, 0)
 
             @pl.when(core == 0)
             def _():
@@ -338,10 +336,6 @@
 
         @pl.when(g == 0)
         def _():
-            @pl.when(last_chip & (core == 1))
-            def _():
-                send_own(1, 0)
-
             @pl.when((core == 1) & (z > 0))
             def _():
                 send_own(1, 1)
@@ -376,6 +370,45 @@
         return 0
 
     lax.fori_loop(0, groups, rest, 0)
+
+    def settle(g, _):
+        for p in range(2):
+            @pl.when(has_next)
+            def _():
+                along(g, 0, p).wait_send()
+
+            @pl.when(has_next & (me >= 2) & jnp.logical_not(last_chip & (g == handed)))
+            def _():
+                along(g, 2, p).wait_send()
+
+            @pl.when(crosses & jnp.logical_not(spared & (g == handed)))
+            def _():
+                across(g, p).wait_send()
+
+            @pl.when(core == 0)
+            def _():
+                beside(g, 0, p).wait_send()
+
+            for lag in (2, 4):
+                @pl.when(me >= lag)
+                def _():
+                    beside(g, lag, p).wait_send()
+        return 0
+
+    lax.fori_loop(0, groups, settle, 0)
+
+    for p in range(2):
+        @pl.when(lends)
+        def _():
+            lend(p).wait_send()
+
+        @pl.when(hands_same)
+        def _():
+            hand_same(p).wait_send()
+
+        @pl.when(hands_other)
+        def _():
+            hand_other(p).wait_send()
 
     def place(refs, frm):
         halves = [ref[...].astype(jnp.float32).reshape(part, per, width) for ref in refs]
@@ -391,46 +424,9 @@
                 device_id=(me, frm), device_id_type=MESH).wait_recv()
         place([rbuf.at[g, frm] for g in range(groups)], frm)
 
-    def settle(g, _):
-        for p in range(2):
-            @pl.when(has_next)
-            def _():
-                along(g, 0, p).wait_send()
-
-            @pl.when(has_next & (me >= 2) & jnp.logical_not(last_chip & (g == handed)))
-            def _():
-                along(g, 2, p).wait_send()
-
-            @pl.when(crosses & jnp.logical_not(spared & (g == handed)))
-            def _():
-                across(g, p).wait_send()
-
-            @pl.when(core == 0)
-            def _():
-                beside(g, 0, p).wait_send()
-
-            for lag in (2, 4):
-                @pl.when(me >= lag)
-                def _():
-                    beside(g, lag, p).wait_send()
+    for g in range(groups):
         for by in range(1, nh):
             give(g, head_at(by)).wait_send()
-        return 0
-
-    lax.fori_loop(0, groups, settle, 0)
-
-    for p in range(2):
-        @pl.when(lends)
-        def _():
-            lend(p).wait_send()
-
-        @pl.when(hands_same)
-        def _():
-            hand_same(p).wait_send()
-
-        @pl.when(hands_other)
-        def _():
-            hand_other(p).wait_send()
 
 
 def local(nc, nh, queries, keys, values, doc_lengths):

time: 34.8 us -> 34.3 us (0.986)
  Pallas kernels: 33.7 us -> 32.9 us
    pallas_call x1, Pallas kernels: 33.7 us -> 32.9 us  [local(): pl.pallas_call(functools.partial(kernel, nc, nh), out_shape=pltpu.VMEM((p...]
where the time goes in v5:
time: 34.3 us; the launch traced here: 33.9 us
  Pallas kernels  32.9 us (96%)
  local copies, waits for them, and re-layouts  0.97 us (3%)
    pallas_call x1, Pallas kernels, local(): pl.pallas_call(functools.partial(kernel, nc, nh), out_shape=pltpu.VMEM((p...  32.9 us
    unnamed x1, local copies, waits for them, and re-layouts  0.97 us

profile of v5, /device:TPU:24, one launch (start us, length us, event | category | flops | bytes accessed | tf_op | source)
XLA Modules:
  0.0 33.9 jit_solution(11130155168604814203)
XLA Ops:
  0.0 32.9 %attend.1 = bf16[64,64,128]{2,1,0:T(8,128)(2,1)S(1)} custom-call(s32[32]{0:T(128)} %dl_hbm.1, bf16[256,16,128]{2,1,0:T(8,128)(2,1)} %q_hbm.1, bf16[512,128]{1,0:T(8,128)(2,1)} %bitcast.2, bf16[512,128]{1,0:T(8,128)(2,1)} %bitcast.3), custom_call_target="tpu_custom_call" | custom-call | tf_op jit(solution)/shard_map/attend/pallas_call | solution.py:440
  32.9 1.0 %copy.6 = bf16[64,64,128]{2,1,0:T(8,128)(2,1)} copy(bf16[64,64,128]{2,1,0:T(8,128)(2,1)S(1)} %attend.1) | data formatting | bytes 2097152

commit v6 on v5

--- a/solution.py
+++ b/solution.py
@@ -50,24 +50,25 @@
         pl.semaphore_signal(barrier, inc=1, device_id=dev, device_id_type=MESH)
 
     has_next = me + 2 < nc
-    crosses = (core == 1) & (me >= 4) & (me + 1 < nc)
 
     z = lax.rem(me // 2, DEEP)
     row_first, row_last = me < 2 * DEEP, me >= nc - 2 * DEEP
     last_chip = (z == DEEP - 1) & jnp.logical_not(row_last)
     first_chip = (z == 0) & jnp.logical_not(row_first)
-    spared = last_chip | first_chip
+    crosses = (core == 1) & (me >= 4) & (me + 1 < nc) & jnp.logical_not(last_chip)
     lends = ((z == DEEP - 2) | ((z == DEEP - 3) & (core == 1))) & jnp.logical_not(row_last)
     hands_same = (z == 3) & jnp.logical_not(row_first)
     hands_other = ((z == 2) | (z == 3)) & (core == 1) & jnp.logical_not(row_first)
     hands = hands_same | hands_other
+    lends_both = (z == DEEP - 3) & lends
+    hands_both = (z == 2) & hands
     handed = groups - 1
 
     @pl.when(me >= 2)
     def _():
         greet((me - 2, mh))
 
-    @pl.when((core == 0) & (me >= 5))
+    @pl.when((core == 0) & (me >= 5) & jnp.logical_not(first_chip))
     def _():
         greet((me - 1, mh))
 
@@ -109,24 +110,25 @@
             send_sem=ss_sem.at[g, lag // 2, p], recv_sem=kr_sem.at[g, there, p],
             device_id=(sib, mh), device_id_type=MESH)
 
-    def lend(p):
-        return pltpu.make_async_remote_copy(
-            src_ref=own.at[handed, p], dst_ref=relay.at[p], send_sem=re_sem.at[0, p], recv_sem=re_sem.at[1, p],
+    def lend(g, p):
+        return pltpu.make_async_remote_copy(
+            src_ref=own.at[g, p], dst_ref=relay.at[g, p], send_sem=re_sem.at[0, g, p], recv_sem=re_sem.at[1, g, p],
             device_id=(me + 10, mh), device_id_type=MESH)
 
     def hand_same(p):
         return pltpu.make_async_remote_copy(
-            src_ref=relay.at[p], dst_ref=kvb.at[handed, 3, p], send_sem=re_sem.at[2, p], recv_sem=kr_sem.at[handed, 3, p],
+            src_ref=relay.at[handed, p], dst_ref=kvb.at[handed, 3, p],
+            send_sem=re_sem.at[2, handed, p], recv_sem=kr_sem.at[handed, 3, p],
             device_id=(me - 6, mh), device_id_type=MESH)
 
-    def hand_other(p):
-        return pltpu.make_async_remote_copy(
-            src_ref=relay.at[p], dst_ref=kvb.at[handed, 4, p], send_sem=re_sem.at[3, p], recv_sem=kr_sem.at[handed, 4, p],
+    def hand_other(g, p):
+        return pltpu.make_async_remote_copy(
+            src_ref=relay.at[g, p], dst_ref=kvb.at[g, 4, p], send_sem=re_sem.at[3, g, p], recv_sem=kr_sem.at[g, 4, p],
             device_id=(me - 5, mh), device_id_type=MESH)
 
-    def relayed(p):
+    def relayed(g, p):
         pltpu.make_async_remote_copy(
-            src_ref=relay.at[p], dst_ref=relay.at[p], send_sem=re_sem.at[0, p], recv_sem=re_sem.at[1, p],
+            src_ref=relay.at[g, p], dst_ref=relay.at[g, p], send_sem=re_sem.at[0, g, p], recv_sem=re_sem.at[1, g, p],
             device_id=(sib, mh), device_id_type=MESH).wait_recv()
 
     def arrive(g, lag, p):
@@ -153,7 +155,7 @@
                 def _():
                     along(g, 2, p).start()
             else:
-                @pl.when(crosses & jnp.logical_not(spared & (g == handed)))
+                @pl.when(crosses & jnp.logical_not(first_chip & (g == handed)))
                 def _():
                     across(g, p).start()
             beside(g, lag, p).start()
@@ -185,10 +187,15 @@
     separate(v_ref, 1)
     send_own(0, 1)
 
+    @pl.when(lends_both)
+    def _():
+        for p in range(2):
+            lend(0, p).start()
+
     @pl.when(lends)
     def _():
         for p in range(2):
-            lend(p).start()
+            lend(handed, p).start()
 
     @pl.when(z == 0)
     def _():
@@ -340,10 +347,16 @@
             def _():
                 send_own(1, 1)
 
+            @pl.when(hands_both)
+            def _():
+                for p in range(2):
+                    relayed(0, p)
+                    hand_other(0, p).start()
+
             @pl.when(hands)
             def _():
                 for p in range(2):
-                    relayed(p)
+                    relayed(handed, p)
 
                     @pl.when(hands_same)
                     def _():
@@ -352,7 +365,7 @@
                 for p in range(2):
                     @pl.when(hands_other)
                     def _():
-                        hand_other(p).start()
+                        hand_other(handed, p).start()
 
         await_lag(g, 3)
         sweep(g, (3, 4), everywhere, False)
@@ -381,7 +394,7 @@
             def _():
                 along(g, 2, p).wait_send()
 
-            @pl.when(crosses & jnp.logical_not(spared & (g == handed)))
+            @pl.when(crosses & jnp.logical_not(first_chip & (g == handed)))
             def _():
                 across(g, p).wait_send()
 
@@ -400,7 +413,11 @@
     for p in range(2):
         @pl.when(lends)
         def _():
-            lend(p).wait_send()
+            lend(handed, p).wait_send()
+
+        @pl.when(lends_both)
+        def _():
+            lend(0, p).wait_send()
 
         @pl.when(hands_same)
         def _():
@@ -408,7 +425,11 @@
 
         @pl.when(hands_other)
         def _():
-            hand_other(p).wait_send()
+            hand_other(handed, p).wait_send()
+
+        @pl.when(hands_both)
+        def _():
+            hand_other(0, p).wait_send()
 
     def place(refs, frm):
         halves = [ref[...].astype(jnp.float32).reshape(part, per, width) for ref in refs]
@@ -456,9 +477,9 @@
             pltpu.VMEM((groups, tiles, 8, TILE), f32),
             pltpu.VMEM((groups, nh, part * per, width), bf),
             pltpu.VMEM((groups, nh, part * per, width), bf),
-            pltpu.VMEM((2, rows, width), bf),
+            pltpu.VMEM((groups, 2, rows, width), bf),
             pltpu.SemaphoreType.DMA((4,)),
-            pltpu.SemaphoreType.DMA((4, 2)),
+            pltpu.SemaphoreType.DMA((4, groups, 2)),
             pltpu.SemaphoreType.DMA((groups, 3, 2)),
             pltpu.SemaphoreType.DMA((groups, 3, 2)),
             pltpu.SemaphoreType.DMA((groups, LAGS - 1, 2)),

time: 34.3 us -> 37.2 us (1.085)
  the two profiles are of different devices: /device:TPU:24 before, /device:TPU:48 now
where the time goes in v6:
time: 37.2 us; the launch traced here: 37.1 us
  Pallas kernels  36.1 us (97%)
  local copies, waits for them, and re-layouts  0.97 us (3%)
    pallas_call x1, Pallas kernels, local(): pl.pallas_call(functools.partial(kernel, nc, nh), out_shape=pltpu.VMEM((p...  36.1 us
    unnamed x1, local copies, waits for them, and re-layouts  0.97 us

profile of v6, /device:TPU:48, one launch (start us, length us, event | category | flops | bytes accessed | tf_op | source)
XLA Modules:
  0.0 37.1 jit_solution(6894836917798926288)
XLA Ops:
  0.0 36.1 %attend.1 = bf16[64,64,128]{2,1,0:T(8,128)(2,1)S(1)} custom-call(s32[32]{0:T(128)} %dl_hbm.1, bf16[256,16,128]{2,1,0:T(8,128)(2,1)} %q_hbm.1, bf16[512,128]{1,0:T(8,128)(2,1)} %bitcast.2, bf16[512,128]{1,0:T(8,128)(2,1)} %bitcast.3), custom_call_target="tpu_custom_call" | custom-call | tf_op jit(solution)/shard_map/attend/pallas_call | solution.py:461
  36.1 1.0 %copy.6 = bf16[64,64,128]{2,1,0:T(8,128)(2,1)} copy(bf16[64,64,128]{2,1,0:T(8,128)(2,1)S(1)} %attend.1) | data formatting | bytes 2097152
